TPU v7x, 32 devices: a whole 2x2x4 slice. The times are simulated.
32 devices in a mesh: slide: 2 (over x), gr: 4 (over y, core), gc: 4 (over z).
Axes of the slice: x: 2, y: 2, z: 4, core: 2. Of those that a mesh axis runs over, the one named last changes fastest.
Arguments:
- features: bfloat16 [128, 32, 512], P(('slide', 'gr'), 'gc'), parts along dimension 0, may hold values from -6 to 6
- out_grad: bfloat16 [128, 32, 512], P(('slide', 'gr'), 'gc'), parts along dimension 0, may hold values from -6 to 6
- w_in: bfloat16 [512, 1024], replicated, may hold values from -0.25 to 0.25
- w_out: bfloat16 [1024, 512], replicated, may hold values from -0.1875 to 0.1875
- decay_row: bfloat16 [128, 32, 1024], P(('slide', 'gr'), 'gc'), parts along dimension 0, may hold values from 0 to 1, as said below
- decay_col: bfloat16 [128, 32, 1024], P(('slide', 'gr'), 'gc'), parts along dimension 0, may hold values from 0 to 1, as said below
- b_proj: float32 [128, 32, 16], P(('slide', 'gr'), 'gc'), parts along dimension 0, may hold values from -6 to 6
- c_proj: float32 [128, 32, 16], P(('slide', 'gr'), 'gc'), parts along dimension 0, may hold values from -6 to 6
- tissue: int32 [128, 32], P(('slide', 'gr'), 'gc'), parts along dimension 0, may hold values from 0 to 1, as said below
Outputs:
- feat_grad: bfloat16 [128, 32, 512], P(('slide', 'gr'), 'gc'), parts along dimension 0
- w_in_grad: float32 [1024, 1024], P('slide'), parts along dimension 0
- w_out_grad: float32 [2048, 512], P('slide'), parts along dimension 0
- decay_row_grad: float32 [128, 32, 1024], P(('slide', 'gr'), 'gc'), parts along dimension 0
- decay_col_grad: float32 [128, 32, 1024], P(('slide', 'gr'), 'gc'), parts along dimension 0
- b_grad: float32 [128, 32, 16], P(('slide', 'gr'), 'gc'), parts along dimension 0
- c_grad: float32 [128, 32, 16], P(('slide', 'gr'), 'gc'), parts along dimension 0
There are 2 independent parts, one for each index of `slide`. A program takes and returns all parts, laid end to end along the dimension named above; an argument that names none is the same for every part. Nothing has to cross between parts.
Inputs may be any that keep to these rules, and one draw needn't show every extreme that they name: 1 marks a tissue tile, 0 background; the share of tissue differs from region to region of the grid. `decay_row`: decays lie in (0, 1], most close to one. `decay_col`: decays lie in (0, 1], most close to one.
All inputs are finite; a program needn't handle non-finite values.
Results may differ from a plain program's by a relative error of at most 0.011.
Values sent between devices are 32-bit elements; how exact they have to be, the bound alone decides.
A program may use at most 128 MiB of HBM per device.

v0:
```python
import math

import jax
import jax.numpy as jnp
from jax import lax
from jax.sharding import PartitionSpec as P


def prefix(part, axis, combine, identity, reverse):
    count = lax.axis_size(axis)
    place = lax.axis_index(axis)
    ahead = count - 1 - place if reverse else place
    gathered = jax.tree.map(lambda a: lax.all_gather(a, axis), part)
    state = jax.tree.map(lambda a, e: jnp.zeros_like(a) + jnp.asarray(e, a.dtype), part, identity)

    def one(turn, state):
        source = count - 1 - turn if reverse else turn
        return combine(
            state, jax.tree.map(lambda a: lax.dynamic_index_in_dim(a, source, 0, False), gathered)
        )

    return lax.fori_loop(0, ahead, one, state)


def chain_pair(earlier, later):
    return (earlier[0] * later[0], later[0][:, None, :] * earlier[1] + later[1])


def chain_identity(totals):
    return (jnp.ones_like(totals[0]), jnp.zeros_like(totals[1]))


def row_entering(totals):
    return prefix(totals, "gc", chain_pair, chain_identity(totals), False)[1]


def row_leaving(totals):
    return prefix(totals, "gc", chain_pair, chain_identity(totals), True)[1]


def block_pass(signal_blk, upstream_blk, row_decay, col_decay, b_proj, c_proj, norm_scale):
    row_count, col_count, inner = signal_blk.shape
    states_n = b_proj.shape[2]
    decay_cols = jnp.moveaxis(row_decay, 1, 0)
    signal_cols = jnp.moveaxis(signal_blk, 1, 0)
    b_cols = jnp.moveaxis(b_proj, 1, 0)

    def row_total_step(carry, inputs):
        product, state = carry
        decay_now, signal_now, b_now = inputs
        source_now = norm_scale * b_now[:, :, None] * signal_now[:, None, :]
        return ((product * decay_now, decay_now[:, None, :] * state + source_now), None)

    start_row = (
        jnp.ones((row_count, inner), jnp.float32),
        jnp.zeros((row_count, states_n, inner), jnp.float32),
    )
    row_totals, unused_row = lax.scan(row_total_step, start_row, (decay_cols, signal_cols, b_cols))
    row_in = row_entering(row_totals)

    def row_emit_step(state, inputs):
        decay_now, signal_now, b_now = inputs
        updated = (
            decay_now[:, None, :] * state + norm_scale * b_now[:, :, None] * signal_now[:, None, :]
        )
        return (updated, updated)

    unused_last, row_state_cols = lax.scan(row_emit_step, row_in, (decay_cols, signal_cols, b_cols))
    row_state = jnp.moveaxis(row_state_cols, 0, 1)

    def col_total_step(carry, inputs):
        product, state = carry
        decay_now, row_now = inputs
        return ((product * decay_now, decay_now[:, None, :] * state + row_now), None)

    start_col = (
        jnp.ones((col_count, inner), jnp.float32),
        jnp.zeros((col_count, states_n, inner), jnp.float32),
    )
    col_totals, unused_col = lax.scan(col_total_step, start_col, (col_decay, row_state))
    col_in = prefix(col_totals, "gr", chain_pair, chain_identity(col_totals), False)[1]

    def col_emit_step(state, inputs):
        decay_now, row_now, c_now, up_now = inputs
        updated = decay_now[:, None, :] * state + row_now
        mixed_now = jnp.sum(c_now[:, :, None] * updated, axis=1)
        c_now_grad = jnp.sum(up_now[:, None, :] * updated, axis=2)
        return (updated, (updated, mixed_now, c_now_grad))

    unused_top, col_outputs = lax.scan(
        col_emit_step, col_in, (col_decay, row_state, c_proj, upstream_blk)
    )
    col_state, mixed, c_part = col_outputs
    col_prev = jnp.concatenate([col_in[None], col_state[:-1]], axis=0)
    col_next = jnp.concatenate([col_decay[1:], jnp.ones_like(col_decay[:1])], axis=0)

    def col_back_total(carry, inputs):
        product, adjoint = carry
        next_now, c_now, up_now = inputs
        injected = c_now[:, :, None] * up_now[:, None, :]
        return ((product * next_now, next_now[:, None, :] * adjoint + injected), None)

    back_totals, unused_back = lax.scan(
        col_back_total, start_col, (col_next, c_proj, upstream_blk), reverse=True
    )
    col_out = (col_decay[0] * back_totals[0], col_decay[0][:, None, :] * back_totals[1])
    col_back = prefix(col_out, "gr", chain_pair, chain_identity(col_out), True)[1]

    def col_back_emit(adjoint, inputs):
        next_now, c_now, up_now, prev_now = inputs
        updated = next_now[:, None, :] * adjoint + c_now[:, :, None] * up_now[:, None, :]
        return (updated, (updated, jnp.sum(updated * prev_now, axis=1)))

    unused_first, back_outputs = lax.scan(
        col_back_emit, col_back, (col_next, c_proj, upstream_blk, col_prev), reverse=True
    )
    col_adj, col_dgrad = back_outputs
    row_next = jnp.concatenate([decay_cols[1:], jnp.ones_like(decay_cols[:1])], axis=0)
    col_adj_cols = jnp.moveaxis(col_adj, 1, 0)
    row_prev_cols = jnp.concatenate([row_in[None], row_state_cols[:-1]], axis=0)

    def row_back_total(carry, inputs):
        product, adjoint = carry
        next_now, adj_now = inputs
        return ((product * next_now, next_now[:, None, :] * adjoint + adj_now), None)

    row_back_totals, unused_rb = lax.scan(
        row_back_total, start_row, (row_next, col_adj_cols), reverse=True
    )
    row_back = row_leaving(
        (decay_cols[0] * row_back_totals[0], decay_cols[0][:, None, :] * row_back_totals[1])
    )

    def row_back_emit(adjoint, inputs):
        next_now, adj_now, prev_now, signal_now, b_now = inputs
        updated = next_now[:, None, :] * adjoint + adj_now
        dgrad_now = jnp.sum(updated * prev_now, axis=1)
        signal_now_part = norm_scale * jnp.sum(b_now[:, :, None] * updated, axis=1)
        b_now_part = norm_scale * jnp.sum(signal_now[:, None, :] * updated, axis=2)
        return (updated, (dgrad_now, signal_now_part, b_now_part))

    unused_rf, row_outputs = lax.scan(
        row_back_emit,
        row_back,
        (row_next, col_adj_cols, row_prev_cols, signal_cols, b_cols),
        reverse=True,
    )
    row_dgrad = jnp.moveaxis(row_outputs[0], 0, 1)
    signal_part = jnp.moveaxis(row_outputs[1], 0, 1)
    b_part = jnp.moveaxis(row_outputs[2], 0, 1)
    return (mixed, signal_part, row_dgrad, col_dgrad, b_part, c_part)


def shards(features, out_grad, w_in, w_out, decay_row, decay_col, b_proj, c_proj, tissue):
    row_count, col_count, model_width = features.shape
    inner = w_in.shape[1]
    grid_cells = row_count * lax.axis_size("gr") * col_count * lax.axis_size("gc")
    norm_scale = 1.0 / math.sqrt(grid_cells)
    feat_rows = features.reshape(row_count * col_count, model_width)
    grad_rows = out_grad.reshape(row_count * col_count, model_width)
    tissue_keep = tissue.astype(jnp.float32)[:, :, None]
    projected = jnp.dot(feat_rows, w_in, preferred_element_type=jnp.float32).reshape(
        row_count, col_count, inner
    )
    signal = (tissue_keep * projected).astype(jnp.bfloat16)
    upstream = lax.dot_general(
        grad_rows, w_out, (((1,), (1,)), ((), ())), preferred_element_type=jnp.float32
    )
    upstream = upstream.reshape(row_count, col_count, inner).astype(jnp.bfloat16)
    mixed_parts, signal_parts, row_parts, col_parts = ([], [], [], [])
    b_grad = jnp.zeros(b_proj.shape, jnp.float32)
    c_grad = jnp.zeros(c_proj.shape, jnp.float32)
    outcome = block_pass(
        signal.astype(jnp.float32),
        upstream.astype(jnp.float32),
        decay_row.astype(jnp.float32),
        decay_col.astype(jnp.float32),
        b_proj,
        c_proj,
        norm_scale,
    )
    mixed_parts.append(outcome[0])
    signal_parts.append(outcome[1])
    row_parts.append(outcome[2])
    col_parts.append(outcome[3])
    b_grad = b_grad + outcome[4]
    c_grad = c_grad + outcome[5]
    mixed = mixed_parts[0].astype(jnp.bfloat16)
    signal_grad = (tissue_keep * signal_parts[0]).astype(jnp.bfloat16)
    grad_flat = signal_grad.reshape(row_count * col_count, inner)
    feat_grad = lax.dot_general(
        grad_flat, w_in, (((1,), (1,)), ((), ())), preferred_element_type=jnp.float32
    )
    feat_grad = feat_grad.astype(jnp.bfloat16).reshape(row_count, col_count, model_width)
    w_in_local = lax.dot_general(
        feat_rows, grad_flat, (((0,), (0,)), ((), ())), preferred_element_type=jnp.float32
    )
    mixed_flat = mixed.reshape(row_count * col_count, inner)
    w_out_local = lax.dot_general(
        mixed_flat, grad_rows, (((0,), (0,)), ((), ())), preferred_element_type=jnp.float32
    )
    w_in_grad, w_out_grad = lax.psum((w_in_local, w_out_local), ("gr", "gc"))
    decay_row_grad = row_parts[0]
    decay_col_grad = col_parts[0]
    return (feat_grad, w_in_grad, w_out_grad, decay_row_grad, decay_col_grad, b_grad, c_grad)


def solution(mesh):
    in_specs = (
        P(("slide", "gr"), "gc", None),
        P(("slide", "gr"), "gc", None),
        P(),
        P(),
        P(("slide", "gr"), "gc", None),
        P(("slide", "gr"), "gc", None),
        P(("slide", "gr"), "gc", None),
        P(("slide", "gr"), "gc", None),
        P(("slide", "gr"), "gc"),
    )
    out_specs = (
        P(("slide", "gr"), "gc", None),
        P("slide", None),
        P("slide", None),
        P(("slide", "gr"), "gc", None),
        P(("slide", "gr"), "gc", None),
        P(("slide", "gr"), "gc", None),
        P(("slide", "gr"), "gc", None),
    )
    return jax.shard_map(shards, mesh=mesh, in_specs=in_specs, out_specs=out_specs, check_vma=False)
```

profile of v0, /device:TPU:0, one launch (start us, length us, event | category | flops | bytes accessed | tf_op | source)
XLA Modules:
  0.0 639.7 jit_solution(3221062963915205826)
XLA Ops:
  11.6 3.2 while.187
  17.6 2.6 fusion.7
  21.0 37.7 %while.186 = (s32[]{:T(128)}, f32[8,1024]{1,0:T(8,128)S(1)}, f32[8,16,1024]{2,1,0:T(8,128)S(1)}, f32[16,8,1024]{2,1,0:T(8,128)}, f32[16,8,16]{2,1,0:T(8,128)}, /...) while((s32[]{:T(128)}, f32[8,1024]{1,0:T(8,128)S(1)}, ...), condition=%wide.region_1.2_spmd.clone, body=%wide.region_0.1_spmd.clone.sunk | while | flops 540676 | bytes 1312384 | solution.py:103
  59.7 18.5 %all-gather.2 = f32[64,1024]{1,0:T(8,128)S(1)} all-gather(f32[16,1024]{1,0:T(8,128)S(1)} %get-tuple-element.996), channel_id=4, replica_groups=mesh['slide'=2,'gr'=4,'gc'=4] {'gc'}, dimensions={0}, use_global_device_ids=true | all-gather | bytes 327680 | tf_op jit(solution)/shard_map/all_gather | solution.py:13
  78.2 25.4 %all-gather.15.cloned.1.call-done = f32[64,16,1024]{2,1,0:T(8,128)} async-done(((f32[16,16,1024]{2,1,0:T(8,128)}), f32[64,16,1024]{2,1,0:T(8,128)}) %all-gather.15.cloned.1.call-update) | async-done | bytes 4194320 | tf_op jit(solution)/shard_map/all_gather | solution.py:13
  103.8 22.9 %while.180 = (s32[]{:T(128)}, f32[16,16,1024]{2,1,0:T(8,128)S(1)}, f32[8,16,16,1024]{3,2,1,0:T(8,128)}, f32[8,16,1024]{2,1,0:T(8,128)}, f32[8,16,16]{2,1,0:T(8,128)}, /*index=5*/f32[8,16,1024]{2,1,0:T(8,128)}, s32[]{:T(128)}) while((s32[]{:T(128)}, f32[16,16,1024]{2,1,0:T(8,128)S(1)}, f32[8,16,16,1024]{3,2,1,0:T(8,128)}, ...), condition=%wide.region_9.10_spmd, body=%wide.region_8.9_spmd.sunk | while | flops 786690 | bytes 3542613 | solution.py:68
  126.7 8.4 %copy.71 = f32[8,16,16,1024]{3,2,0,1:T(8,128)} copy(f32[8,16,16,1024]{3,2,1,0:T(8,128)} %get-tuple-element.999) | data formatting | bytes 16777216 | tf_op jit(solution)/shard_map/while | solution.py:68
  135.1 33.2 %while.188 = (s32[]{:T(128)}, f32[8,1024]{1,0:T(8,128)S(1)}, f32[8,16,1024]{2,1,0:T(8,128)S(1)}, f32[16,8,1024]{2,1,0:T(8,128)}, f32[16,8,16,1024]{3,2,1,0:T(8,128)}, /*index=5*/s32[]{:T(128)}, s32[]{:T(128)}) while((s32[]{:T(128)}, f32[8,1024]{1,0:T(8,128)S(1)}, f32[8,16,1024]{2,1,0:T(8,128)S(1)}, f32[16,8,1024]{2,1,0:T(8,128)}, ...), condition=%wide.region_11.12_spmd.clone, body=%wide.region_10.11_spmd.clone.sunk | while | flops 409603 | bytes 1736800 | solution.py:80
  170.9 5.4 all-gather
  177.1 4.0 while.178
  181.2 6.1 all-gather.4
  187.3 9.1 %all-gather.17.cloned.1.call-done = f32[32,16,1024]{2,1,0:T(8,128)} async-done(((f32[8,16,1024]{2,1,0:T(8,128)}), f32[32,16,1024]{2,1,0:T(8,128)}) %all-gather.17.cloned.1.call-update) | async-done | bytes 2097168 | tf_op jit(solution)/shard_map/all_gather | solution.py:13
  198.3 79.2 %while.182 = (s32[]{:T(128)}, f32[8,16,1024]{2,1,0:T(8,128)S(1)}, f32[16,8,16,1024]{3,2,1,0:T(8,128)}, bf16[16,8,1024]{2,1,0:T(8,128)(2,1)}, f32[16,8,16]{2,1,0:...) while((s32[]{:T(128)}, f32[8,16,1024]{2,1,0:T(8,128)S(1)}, ...), condition=%wide.region_17.18_spmd, body=%wide.region_14.17_spmd.sunk | while | flops 778114 | bytes 2875505 | solution.py:90
  199.7 1.4 multiply_reduce_fusion.6
  204.7 1.4 multiply_reduce_fusion.6
  209.7 1.4 multiply_reduce_fusion.6
  214.6 1.4 multiply_reduce_fusion.6
  219.5 1.4 multiply_reduce_fusion.6
  224.5 1.4 multiply_reduce_fusion.6
  229.4 1.4 multiply_reduce_fusion.6
  234.4 1.4 multiply_reduce_fusion.6
  239.3 1.4 multiply_reduce_fusion.6
  244.3 1.4 multiply_reduce_fusion.6
  249.2 1.4 multiply_reduce_fusion.6
  254.1 1.4 multiply_reduce_fusion.6
  259.1 1.4 multiply_reduce_fusion.6
  264.0 1.4 multiply_reduce_fusion.6
  269.0 1.4 multiply_reduce_fusion.6
  277.4 4.1 slice.24
  281.5 4.1 pad_maximum_fusion
  285.6 4.3 broadcast.84.clone
  290.0 57.4 %while.183 = (s32[]{:T(128)}, f32[8,16,1024]{2,1,0:T(8,128)S(1)}, f32[16,8,16,1024]{3,2,0,1:T(8,128)}, f32[16,8,1024]{2,1,0:T(8,128)S(1)}, f32[16,8,1024]{2,1,0:...) while((s32[]{:T(128)}, f32[8,16,1024]{2,1,0:T(8,128)S(1)}, ...), condition=%wide.region_20.21_spmd, body=%wide.region_18.20_spmd.sunk | while | flops 647171 | bytes 2918021 | solution.py:114
  348.2 29.1 %while.189 = (s32[]{:T(128)}, f32[16,1024]{1,0:T(8,128)S(1)}, f32[16,16,1024]{2,1,0:T(8,128)}, f32[8,16,1024]{2,1,0:T(8,128)}, f32[8,16,16,1024]{3,2,1,0:T(8,128)}, /*index=5*/s32[]{:T(128)}, s32[]{:T(128)}, s32[]{:T(128)}) while((s32[]{:T(128)}, f32[16,1024]{1,0:T(8,128)S(1)}, f32[16,16,1024]{2,1,0:T(8,128)}, ...), condition=%wide.region_22.23_spmd.clone, body=%wide.region_21.22_spmd.clone.sunk | while | flops 819204 | bytes 3473524 | solution.py:127
  349.1 2.5 bitcast_add_fusion.21
  352.4 2.8 bitcast_add_fusion.21
  356.1 2.8 bitcast_add_fusion.21
  359.8 2.8 bitcast_add_fusion.21
  363.5 2.8 bitcast_add_fusion.21
  367.1 2.8 bitcast_add_fusion.21
  370.8 2.8 bitcast_add_fusion.21
  374.5 2.8 bitcast_add_fusion.21
  377.3 2.3 broadcast_multiply_fusion.1
  379.8 3.8 slice.25
  383.6 4.2 pad_maximum_fusion.1
  388.6 16.8 %all-gather.6 = f32[64,1024]{1,0:T(8,128)S(1)} all-gather(f32[16,1024]{1,0:T(8,128)S(1)} %fusion.17), channel_id=8, replica_groups=mesh['slide'=2,'gr'=4,'gc'=4] {'gc'}, dimensions={0}, use_global_device_ids=true | all-gather | bytes 327680 | tf_op jit(solution)/shard_map/all_gather | solution.py:13
  405.5 1.8 convolution_bitcast_fusion
  407.3 60.0 %all-gather.19.cloned.1.call-done = f32[64,16,1024]{2,1,0:T(8,128)} async-done(((f32[16,16,1024]{2,1,0:T(8,128)}), f32[64,16,1024]{2,1,0:T(8,128)}) %all-gather.19.cloned.1.call-update) | async-done | bytes 4194320 | tf_op jit(solution)/shard_map/all_gather | solution.py:13
  467.3 5.5 while.184
  467.6 1.7 bitcast_add_fusion.19
  469.3 1.7 bitcast_add_fusion.19
  471.1 1.7 bitcast_add_fusion.19
  473.0 40.8 %while.185 = (s32[]{:T(128)}, f32[16,16,1024]{2,1,0:T(8,128)S(1)}, f32[8,16,1024]{2,0,1:T(8,128)S(1)}, f32[8,16,1024]{2,0,1:T(8,128)S(1)}, f32[8,16,16]{2,0,1:T(...) while((s32[]{:T(128)}, f32[16,16,1024]{2,1,0:T(8,128)S(1)}, ...), condition=%wide.region_29.30_spmd, body=%wide.region_25.29_spmd.sunk | while | flops 2080771 | bytes 5382305 | solution.py:142
  474.6 2.3 multiply_reduce_fusion.7
  479.7 2.3 multiply_reduce_fusion.7
  484.8 2.3 multiply_reduce_fusion.7
  489.9 2.3 multiply_reduce_fusion.7
  495.0 2.3 multiply_reduce_fusion.7
  500.1 2.3 multiply_reduce_fusion.7
  505.2 2.3 multiply_reduce_fusion.7
  510.3 2.3 multiply_reduce_fusion.7
  513.8 1.9 convolution_bitcast_fusion.1
  516.8 110.4 %all-reduce.5.cloned.1.call-done = (f32[512,1024]{0,1:T(8,128)}, f32[1024,512]{1,0:T(8,128)}) async-done(((f32[512,1024]{0,1:T(8,128)}, f32[1024,512]{1,0:T(8,128)}), (f32[512,1024]{0,1:T(8,128)}, f32[1024,512]{1,0:T(8,128)})) %all-reduce.5.cloned.1.call-update) | async-done | bytes 4194320 | tf_op jit(solution)/shard_map/psum | solution.py:202
  627.2 2.9 copy.59
  630.1 3.1 copy.199
  (489 shorter events, 260.7 us)
Async XLA Ops:
  7.2 2.0 copy-start
  7.2 96.4 %all-gather.15.cloned.1.call-start = ((), (), s32[]{:S(2)}) async-start(), calls=%async_computation.1 | async-start | bytes 5242880 | tf_op jit(solution)/shard_map/all_gather | solution.py:13
  9.2 6.7 %copy-start.9 = (bf16[16,8,1024]{2,1,0:T(8,128)(2,1)S(1)}, bf16[16,8,1024]{2,1,0:T(8,128)(2,1)}, u32[]{:S(2)}) copy-start(bf16[16,8,1024]{2,1,0:T(8,128)(2,1)} %param.38) | copy-start | bytes 786436
  14.8 1.0 copy-start.1
  14.8 1.9 copy-start.10
  14.9 88.8 %copy-start.6 = (f32[8,16,1024]{2,1,0:T(8,128)}, f32[8,16,1024]{2,1,0:T(8,128)S(1)}, u32[]{:S(2)}) copy-start(f32[8,16,1024]{2,1,0:T(8,128)S(1)} %get-tuple-element.2221) | copy-start | bytes 1572868
  14.9 88.8 %copy-start.8 = (f32[8,16,1024]{2,1,0:T(8,128)}, f32[8,16,1024]{2,1,0:T(8,128)S(1)}, u32[]{:S(2)}) copy-start(f32[8,16,1024]{2,1,0:T(8,128)S(1)} %get-tuple-element.2223) | copy-start | bytes 1572868
  15.8 161.2 %all-gather.13.cloned.1.call-start = ((), (), s32[]{:S(2)}) async-start(), calls=%async_computation | async-start | bytes 2621440 | tf_op jit(solution)/shard_map/all_gather | solution.py:13
  59.6 136.7 %all-gather.17.cloned.1.call-start = ((), (), s32[]{:S(2)}) async-start(), calls=%async_computation.2 | async-start | bytes 2621440 | tf_op jit(solution)/shard_map/all_gather | solution.py:13
  126.7 8.4 %copy-start.4 = (f32[8,16,1024]{2,1,0:T(8,128)S(1)}, f32[8,16,1024]{2,1,0:T(8,128)}, u32[]{:S(2)}) copy-start(f32[8,16,1024]{2,1,0:T(8,128)} %custom-call.5) | copy-start | bytes 1572868
  135.1 34.1 %copy-start.7 = (f32[8,16,1024]{2,1,0:T(8,128)S(1)}, f32[8,16,1024]{2,1,0:T(8,128)}, u32[]{:S(2)}) copy-start(f32[8,16,1024]{2,1,0:T(8,128)} %get-tuple-element.2222) | copy-start | bytes 1572868
  168.3 0.8 copy-start.5
  169.2 298.1 %all-gather.19.cloned.1.call-start = ((), (), s32[]{:S(2)}) async-start(), calls=%async_computation.3 | async-start | bytes 5242880 | tf_op jit(solution)/shard_map/all_gather | solution.py:13
  196.4 0.8 copy-start.2
  277.4 4.1 copy-start.3
  347.4 0.8 copy-start.12
  379.6 247.6 %all-reduce.5.cloned.1.call-start = ((), (), s32[]{:S(2)}) async-start(), calls=%async_computation.4 | async-start | bytes 8388608 | tf_op jit(solution)/shard_map/psum | solution.py:202
  383.6 21.9 %copy-start.13 = (bf16[16,8,1024]{2,1,0:T(8,128)(2,1)S(1)}, bf16[16,8,1024]{2,1,0:T(8,128)(2,1)}, u32[]{:S(2)}) copy-start(bf16[16,8,1024]{2,1,0:T(8,128)(2,1)} %get-tuple-element.1009) | copy-start | bytes 786436
  383.6 21.9 %copy-start.14 = (bf16[16,8,512]{2,1,0:T(8,128)(2,1)S(1)}, bf16[16,8,512]{2,1,0:T(8,128)(2,1)}, u32[]{:S(2)}) copy-start(bf16[16,8,512]{2,1,0:T(8,128)(2,1)} %param.34) | copy-start | bytes 393220
  472.9 40.8 %copy-start.15 = (bf16[16,8,512]{2,1,0:T(8,128)(2,1)S(1)}, bf16[16,8,512]{2,1,0:T(8,128)(2,1)}, u32[]{:S(2)}) copy-start(bf16[16,8,512]{2,1,0:T(8,128)(2,1)} %param.33) | copy-start | bytes 393220
  513.7 1.9 copy-start.11
  513.8 1.9 copy-start.16
Sparse Core Ops, SparseCore 0:
  15.9 87.5 all-gather.14
  105.1 21.1 all-gather.12
  169.3 26.9 all-gather.16
  379.8 87.4 all-gather.18
  515.8 111.3 all-reduce.4
where the time goes:
time: 652 us; the launch traced here: 640 us
  waiting for transfers between devices  205 us (31%)
  other arithmetic  182 us (28%)
  local copies, waits for them, and re-layouts  181 us (28%)
  blocking collectives  46.9 us (7%)
  between operations  14.2 us (2%)
  matrix products  8.64 us (1%)
    psum x1, waiting for transfers between devices, shards(): w_in_grad, w_out_grad = lax.psum((w_in_local, w_out_local), ('gr', 'gc'))  110 us
    all_gather x4, waiting for transfers between devices, prefix(): gathered = jax.tree.map(lambda a: lax.all_gather(a, axis), part)  94.4 us
    all_gather x4, blocking collectives, prefix(): gathered = jax.tree.map(lambda a: lax.all_gather(a, axis), part)  46.9 us
    dynamic_update_slice x80, local copies, waits for them, and re-layouts, block_pass(): lax.scan(col_emit_step, col_in, (col_decay, row_state, c_proj, upstream_b...  46.4 us
    mul x32, local copies, waits for them, and re-layouts, col_back_emit(): c_now[:, :, None] * up_now[:, None, :]  23.5 us
    mul x32, local copies, waits for them, and re-layouts, col_back_total(): injected = c_now[:, :, None] * up_now[:, None, :]  23.2 us
    reduce_sum x16, other arithmetic, col_emit_step(): c_now_grad = jnp.sum(up_now[:, None, :] * updated, axis=2)  22.9 us
    add x8, other arithmetic, row_back_total(): next_now[:, None, :] * adjoint + adj_now  22.2 us
  transfers between devices with their start and end apart: 5, of which 4 were waited for; matrix products, arithmetic and copies ran while one was open for 20% of the time, Pallas kernels for 0%

commit v1 on v0

v1 whole, which is shorter than its diff:
```python
import functools
import math

import jax
import jax.numpy as jnp
from jax import lax
from jax.experimental import pallas as pl
from jax.experimental.pallas import tpu as pltpu
from jax.sharding import PartitionSpec as P

LANES = 128
F32 = jnp.float32


def place(shape):
    return lax.broadcasted_iota(jnp.int32, shape, 0)


def ahead_weights(decay):
    count = decay.shape[0]
    where = place(decay.shape)
    product, steps, shift = decay, [], 1
    while shift < count:
        inside = where >= shift
        steps.append((shift, jnp.where(inside, product, 0.0)))
        product = jnp.where(inside, product * pltpu.roll(product, shift, 0), product)
        shift *= 2
    return steps, product


def back_weights(decay):
    count = decay.shape[0]
    where = place(decay.shape)
    product = jnp.where(where == count - 1, 1.0, pltpu.roll(decay, count - 1, 0))
    steps, shift = [], 1
    while shift < count:
        inside = where < count - shift
        steps.append((count - shift, jnp.where(inside, product, 0.0)))
        product = jnp.where(inside, product * pltpu.roll(product, count - shift, 0), product)
        shift *= 2
    return steps, product


def run_scan(steps, value):
    for shift, weight in steps:
        value = value + weight * pltpu.roll(value, shift, 0)
    return value


def spread(source_ref, target_ref, scale):
    rows, cols, states = source_ref.shape

    def one(i, carry):
        block = source_ref[i] * scale
        for n in range(states):
            target_ref[i, n] = jnp.broadcast_to(block[:, n : n + 1], (cols, LANES))
        return carry

    lax.fori_loop(0, rows, one, 0)


def totals_kernel(scale, signal, upstream, row_decay, col_decay, b_proj, c_proj,
                  row_tot, row_prod, col_tot, col_prod, b_wide, c_wide):
    rows, cols, states = b_proj.shape

    @pl.when(pl.program_id(0) == 0)
    def _():
        spread(b_proj, b_wide, scale)
        spread(c_proj, c_wide, 1.0)

    def one(turn, carry):
        i = rows - 1 - turn
        product, adjoints = carry[0], carry[1:]
        down = col_decay[i]
        up = upstream[i]
        suffix = back_weights(row_decay[i])[1]
        weighted = suffix * signal[i]
        updated = []
        for n in range(states):
            updated.append(down * (adjoints[n] + c_wide[i, n] * up))
            row_tot[i, n : n + 1, :] = jnp.sum(b_wide[i, n] * weighted, axis=0, keepdims=True)
        row_prod[i] = row_decay[i][0:1] * suffix[0:1]
        return (product * down, *updated)

    ones = jnp.ones((cols, LANES), F32)
    zeros = jnp.zeros((cols, LANES), F32)
    out = lax.fori_loop(0, rows, one, (ones,) + (zeros,) * states)
    col_prod[...] = out[0]
    for n in range(states):
        col_tot[n] = out[1 + n]


def states_kernel(scale, signal, upstream, row_decay, col_decay, b_proj, c_proj, row_in, back_in,
                  row_state, col_adj, col_tot, back_tot, b_wide, c_wide):
    rows, cols, states = b_proj.shape

    @pl.when(pl.program_id(0) == 0)
    def _():
        spread(b_proj, b_wide, scale)
        spread(c_proj, c_wide, 1.0)

    def back(turn, entering):
        i = rows - 1 - turn
        down = col_decay[i]
        up = upstream[i]
        prefix_weight = ahead_weights(row_decay[i])[1]
        updated = []
        for n in range(states):
            adjoint = entering[n] + c_wide[i, n] * up
            col_adj[i, n] = adjoint
            back_tot[i, n : n + 1, :] = jnp.sum(prefix_weight * adjoint, axis=0, keepdims=True)
            updated.append(down * adjoint)
        return tuple(updated)

    lax.fori_loop(0, rows, back, tuple(back_in[n] for n in range(states)))

    def ahead(i, column):
        down = col_decay[i]
        source = signal[i]
        steps, product = ahead_weights(row_decay[i])
        updated = []
        for n in range(states):
            state = run_scan(steps, b_wide[i, n] * source) + product * row_in[i, n : n + 1, :]
            row_state[i, n] = state
            updated.append(down * column[n] + state)
        return tuple(updated)

    zeros = jnp.zeros((cols, LANES), F32)
    out = lax.fori_loop(0, rows, ahead, (zeros,) * states)
    for n in range(states):
        col_tot[n] = out[n]


def outputs_kernel(scale, signal, upstream, row_decay, col_decay, b_proj, c_proj,
                   row_state, col_adj, row_in, col_in, row_back,
                   mixed, signal_part, row_grad, col_grad, b_grad, c_grad,
                   b_wide, c_wide, b_sum, c_sum):
    rows, cols, states = b_proj.shape

    @pl.when(pl.program_id(0) == 0)
    def _():
        spread(b_proj, b_wide, scale)
        spread(c_proj, c_wide, 1.0)
        b_sum[...] = jnp.zeros_like(b_sum)
        c_sum[...] = jnp.zeros_like(c_sum)

    def one(i, column):
        down = col_decay[i]
        source = signal[i]
        up = upstream[i]
        steps, product = back_weights(row_decay[i])
        first = place((cols, LANES)) == 0
        mixed_now = jnp.zeros((cols, LANES), F32)
        signal_now, row_now, col_now = mixed_now, mixed_now, mixed_now
        updated = []
        for n in range(states):
            state = row_state[i, n]
            adjoint = col_adj[i, n]
            col_now = col_now + adjoint * column[n]
            fresh = down * column[n] + state
            updated.append(fresh)
            mixed_now = mixed_now + c_wide[i, n] * fresh
            c_sum[i, n] += up * fresh
            row_adj = run_scan(steps, adjoint) + product * row_back[i, n : n + 1, :]
            before = jnp.where(first, row_in[i, n : n + 1, :], pltpu.roll(state, 1, 0))
            row_now = row_now + row_adj * before
            signal_now = signal_now + b_wide[i, n] * row_adj
            b_sum[i, n] += source * row_adj
        mixed[i] = mixed_now
        signal_part[i] = signal_now
        row_grad[i] = row_now
        col_grad[i] = col_now
        return tuple(updated)

    lax.fori_loop(0, rows, one, tuple(col_in[n] for n in range(states)))

    @pl.when(pl.program_id(0) == pl.num_programs(0) - 1)
    def _():
        def finish(i, carry):
            for n in range(states):
                b_grad[i, :, n : n + 1] = scale * jnp.sum(b_sum[i, n], axis=1, keepdims=True)
                c_grad[i, :, n : n + 1] = jnp.sum(c_sum[i, n], axis=1, keepdims=True)
            return carry

        lax.fori_loop(0, rows, finish, 0)


def tile(shape):
    zeros = (0,) * (len(shape) - 1)
    return pl.BlockSpec((*shape[:-1], LANES), lambda t: (*zeros, t))


def whole(shape):
    zeros = (0,) * len(shape)
    return pl.BlockSpec(shape, lambda t: zeros)


def call(kernel, name, scale, args, kept, outs, kept_outs, scratch):
    return pl.pallas_call(
        functools.partial(kernel, scale),
        grid=(args[0].shape[-1] // LANES,),
        in_specs=[whole(a.shape) if k in kept else tile(a.shape) for k, a in enumerate(args)],
        out_specs=[whole(o) if k in kept_outs else tile(o) for k, o in enumerate(outs)],
        out_shape=[jax.ShapeDtypeStruct(o, F32) for o in outs],
        scratch_shapes=[pltpu.VMEM(s, F32) for s in scratch],
        compiler_params=pltpu.CompilerParams(vmem_limit_bytes=40 * 2**20),
        name=name,
    )(*args)


def entering(total, product, axis, reverse):
    count = lax.axis_size(axis)
    me = lax.axis_index(axis)
    totals = lax.all_gather(total, axis)
    products = lax.all_gather(product, axis)
    state = jnp.zeros_like(total)
    for turn in range(count - 1):
        k = count - 1 - turn if reverse else turn
        use = k > me if reverse else k < me
        state = jnp.where(use, products[k] * state + totals[k], state)
    return state


def shards(features, out_grad, w_in, w_out, decay_row, decay_col, b_proj, c_proj, tissue):
    rows, cols, width = features.shape
    inner = w_in.shape[1]
    states = b_proj.shape[2]
    cells = rows * cols
    scale = 1.0 / math.sqrt(cells * lax.axis_size("gr") * lax.axis_size("gc"))
    feat = features.reshape(cells, width)
    grad = out_grad.reshape(cells, width)
    keep = tissue.astype(F32)[:, :, None]
    contract_last = (((1,), (1,)), ((), ()))
    contract_first = (((0,), (0,)), ((), ()))
    projected = jnp.dot(feat, w_in, preferred_element_type=F32).reshape(rows, cols, inner)
    signal = (keep * projected).astype(jnp.bfloat16).astype(F32)
    upstream = lax.dot_general(grad, w_out, contract_last, preferred_element_type=F32)
    upstream = upstream.astype(jnp.bfloat16).astype(F32).reshape(rows, cols, inner)
    common = (signal, upstream, decay_row.astype(F32), decay_col.astype(F32), b_proj, c_proj)

    cell = (rows, cols, inner)
    row_edge = (rows, states, inner)
    col_edge = (states, cols, inner)
    full = (rows, states, cols, inner)
    wide = (rows, states, cols, LANES)
    row_tot, row_prod, col_back_tot, col_prod = call(
        totals_kernel, "totals", scale, common, (4, 5),
        (row_edge, (rows, 1, inner), col_edge, (cols, inner)), (), (wide, wide),
    )
    row_in = entering(row_tot, row_prod, "gc", False)
    col_back = entering(col_back_tot, col_prod, "gr", True)
    row_state, col_adj, col_tot, row_back_tot = call(
        states_kernel, "states", scale, (*common, row_in, col_back), (4, 5),
        (full, full, col_edge, row_edge), (), (wide, wide),
    )
    col_in = entering(col_tot, col_prod, "gr", False)
    row_back = entering(row_back_tot, row_prod, "gc", True)
    mixed, signal_part, row_grad, col_grad, b_grad, c_grad = call(
        outputs_kernel, "outputs", scale,
        (*common, row_state, col_adj, row_in, col_in, row_back), (4, 5),
        (cell, cell, cell, cell, b_proj.shape, c_proj.shape), (4, 5), (wide, wide, wide, wide),
    )
    mixed = mixed.astype(jnp.bfloat16).reshape(cells, inner)
    signal_grad = (keep * signal_part).astype(jnp.bfloat16).reshape(cells, inner)
    feat_grad = lax.dot_general(signal_grad, w_in, contract_last, preferred_element_type=F32)
    feat_grad = feat_grad.astype(jnp.bfloat16).reshape(rows, cols, width)
    w_in_part = lax.dot_general(feat, signal_grad, contract_first, preferred_element_type=F32)
    w_out_part = lax.dot_general(mixed, grad, contract_first, preferred_element_type=F32)
    w_in_grad, w_out_grad = lax.psum((w_in_part, w_out_part), ("gr", "gc"))
    return (feat_grad, w_in_grad, w_out_grad, row_grad, col_grad, b_grad, c_grad)


def solution(mesh):
    cell = P(("slide", "gr"), "gc", None)
    in_specs = (cell, cell, P(), P(), cell, cell, cell, cell, P(("slide", "gr"), "gc"))
    out_specs = (cell, P("slide", None), P("slide", None), cell, cell, cell, cell)
    return jax.shard_map(shards, mesh=mesh, in_specs=in_specs, out_specs=out_specs, check_vma=False)
```

time: 652 us -> 409 us (0.63); the launches traced: 640 us -> 409 us
  other arithmetic: 182 us -> 13.7 us
  local copies, waits for them, and re-layouts: 181 us -> 18.2 us
  waiting for transfers between devices: 205 us -> 293 us
  Pallas kernels: 0 us -> 41.6 us
  blocking collectives: 46.9 us -> 21.8 us
    mul x135 -> x0, local copies, waits for them, and re-layouts: 90.2 us -> none  [the longest x32 23.5 us: col_back_emit(): c_now[:, :, None] * up_now[:, None, :]]
    all_gather x4, waiting for transfers between devices: 94.4 us -> 183 us  [entering(): totals = lax.all_gather(total, axis)]
    reduce_sum x40 -> x0, other arithmetic: 61.6 us -> none  [the longest x16 22.9 us: col_emit_step(): c_now_grad = jnp.sum(up_now[:, None, :] * updated, axis=2)]
    add x54 -> x0, other arithmetic: 56.1 us -> none  [the longest x8 22.2 us: row_back_total(): next_now[:, None, :] * adjoint + adj_now]
    dynamic_update_slice x120 -> x0, local copies, waits for them, and re-layouts: 55.1 us -> none  [the longest x80 46.4 us: block_pass(): lax.scan(col_emit_step, col_in, (col_decay, row_state, c_proj, upstream_b...]
    pallas_call x0 -> x3, Pallas kernels: none -> 41.6 us  [call(): pl.pallas_call(functools.partial(kernel, scale), grid=(args[0].shape[-1]...]
    mul x84 -> x2, other arithmetic: 42.3 us -> 1.41 us  [entering(): state = jnp.where(use, products[k] * state + totals[k], state)]
    all_gather x4 -> x2, blocking collectives: 46.9 us -> 21.8 us  [entering(): products = lax.all_gather(product, axis)]
  transfers between devices with their start and end apart: 5 -> 5, of which waited for: 4 -> 5; matrix products, arithmetic and copies ran while one was open for 20% -> 2% of each run, Pallas kernels for 0% -> 0%
where the time goes in v1:
time: 409 us
  waiting for transfers between devices  293 us (72%)
  Pallas kernels  41.6 us (10%)
  blocking collectives  21.8 us (5%)
  local copies, waits for them, and re-layouts  18.2 us (4%)
  between operations  14.1 us (3%)
  other arithmetic  13.7 us (3%)
  matrix products  6.5 us (2%)
    all_gather x4, waiting for transfers between devices, entering(): totals = lax.all_gather(total, axis)  183 us
    psum x1, waiting for transfers between devices, shards(): w_in_grad, w_out_grad = lax.psum((w_in_part, w_out_part), ('gr', 'gc'))  108 us
    pallas_call x3, Pallas kernels, call(): pl.pallas_call(functools.partial(kernel, scale), grid=(args[0].shape[-1]...  41.6 us
    all_gather x2, blocking collectives, entering(): products = lax.all_gather(product, axis)  21.8 us
    unnamed x51, local copies, waits for them, and re-layouts  18.1 us
    select_n x4, other arithmetic, entering(): state = jnp.where(use, products[k] * state + totals[k], state)  9.46 us
  transfers between devices with their start and end apart: 5, of which 5 were waited for; matrix products, arithmetic and copies ran while one was open for 2% of the time, Pallas kernels for 0%

profile of v1, /device:TPU:0, one launch (start us, length us, event | category | flops | bytes accessed | tf_op | source)
XLA Modules:
  0.0 408.7 jit_solution(13295074424810765663)
XLA Ops:
  7.2 0.0 copy-start
  7.2 0.0 copy-start.20
  7.2 0.0 all-gather.13.cloned.1.call-start
  7.2 0.8 convert_element_type.28
  8.0 0.1 copy.22
  8.1 1.1 convert_element_type.32.row_decay
  9.2 0.0 copy-start.13
  9.2 0.0 copy-start.14
  9.2 1.0 convert_element_type.33.col_decay
  10.2 0.0 copy-done.19
  10.2 1.4 fusion.3.upstream
  11.6 0.0 copy-done
  11.6 0.0 copy-done.20
  11.6 0.0 copy-start.3
  11.7 0.3 fusion.1.signal
  12.0 0.0 copy-done.13
  12.0 0.0 copy-done.14
  12.0 0.0 copy-start.6
  12.0 8.1 %totals.1 = (f32[16,16,1024]{2,1,0:T(8,128)S(1)}, f32[16,1,1024]{2,1,0:T(1,128)S(1)}, f32[16,8,1024]{2,1,0:T(8,128)S(1)}, f32[8,1024]{1,0:T(8,128)S(1)}) custom-call(f32[16,8,1024]{2,1,0:T(8,128)S(1)} %fusion.1.signal, f32[16,8,1024]{2,1,0:T(8,128)S(1)} %fusion.3.upstream, f32[16,8,1024]{2,1,0:T(8,128)S(1)} %convert_element_type.32.row_decay, ...), custom_call_target="tpu_custom_call" | custom-call | tf_op jit(solution)/shard_map/totals/pallas_call | solution.py:199
  20.1 0.0 copy-start.11
  20.1 1.0 copy-done.11
  21.1 0.8 copy-done.15
  21.9 0.0 all-gather.13.cloned.1.call-update
  21.9 0.0 copy-done.3
  21.9 0.0 all-gather.11.cloned.1.call-start
  22.0 0.7 all-gather.11.cloned.1.call-update
  22.7 0.0 all-gather.15.cloned.1.call-start
  22.7 15.6 %all-gather = f32[64,1,1024]{2,1,0:T(1,128)S(1)} all-gather(f32[16,1,1024]{2,1,0:T(1,128)S(1)} %get-tuple-element.21), channel_id=2, replica_groups=mesh['slide'=2,'gr'=4,'gc'=4] {'gc'}, dimensions={0}, use_global_device_ids=true | all-gather | bytes 327680 | tf_op jit(solution)/shard_map/all_gather | solution.py:215
  38.4 0.8 slice_multiply_fusion
  39.1 0.0 copy-done.6
  39.2 6.2 %all-gather.2 = f32[32,1024]{1,0:T(8,128)S(1)} all-gather(f32[8,1024]{1,0:T(8,128)S(1)} %get-tuple-element.23), channel_id=4, replica_groups=mesh['slide'=2,'gr'=4,'gc'=4] {'gr'}, dimensions={0}, use_global_device_ids=true | all-gather | bytes 163840 | tf_op jit(solution)/shard_map/all_gather | solution.py:215
  45.4 0.6 slice_multiply_fusion.2
  46.0 2.0 all-gather.13.cloned.1.call-done
  48.0 2.3 fusion.15.back_in
  50.4 80.6 %all-gather.11.cloned.1.call-done = f32[64,16,1024]{2,1,0:T(8,128)} async-done(((f32[16,16,1024]{2,1,0:T(8,128)}), f32[64,16,1024]{2,1,0:T(8,128)}) %all-gather.11.cloned.1.call-update) | async-done | bytes 4194320 | tf_op jit(solution)/shard_map/all_gather | solution.py:214
  131.0 2.4 fusion.8.row_in
  133.4 0.0 copy-done.4
  133.4 0.0 copy-done.7
  133.4 0.0 copy-done.9
  133.4 15.9 %states.1 = (f32[16,16,8,1024]{3,2,1,0:T(8,128)S(1)}, f32[16,16,8,1024]{3,2,1,0:T(8,128)}, f32[16,8,1024]{2,1,0:T(8,128)S(1)}, f32[16,16,1024]{2,1,0:T(8,128)S(1)}) custom-call(f32[16,8,1024]{2,1,0:T(8,128)S(1)} %copy-done.7, f32[16,8,1024]{2,1,0:T(8,128)S(1)} %copy-done.4, f32[16,8,1024]{2,1,0:T(8,128)S(1)} %convert_element_type.32.row_decay, ...), custom_call_target="tpu_custom_call" | custom-call | tf_op jit(solution)/shard_map/states/pallas_call | solution.py:199
  149.3 3.2 copy-done.1
  152.5 1.0 copy-done.12
  153.5 0.8 copy-done.16
  154.3 0.0 all-gather.15.cloned.1.call-update
  154.3 0.0 all-gather.17.cloned.1.call-start
  154.4 0.5 all-gather.17.cloned.1.call-update
  154.9 0.0 all-reduce.3.cloned.1.call-start
  155.0 0.9 copy.40
  155.8 19.8 %all-gather.15.cloned.1.call-done = f32[64,8,1024]{2,1,0:T(8,128)} async-done(((f32[16,8,1024]{2,1,0:T(8,128)}), f32[64,8,1024]{2,1,0:T(8,128)}) %all-gather.15.cloned.1.call-update) | async-done | bytes 2097168 | tf_op jit(solution)/shard_map/all_gather | solution.py:214
  175.6 2.3 fusion.12.col_in
  177.9 80.5 %all-gather.17.cloned.1.call-done = f32[64,16,1024]{2,1,0:T(8,128)} async-done(((f32[16,16,1024]{2,1,0:T(8,128)}), f32[64,16,1024]{2,1,0:T(8,128)}) %all-gather.17.cloned.1.call-update) | async-done | bytes 4194320 | tf_op jit(solution)/shard_map/all_gather | solution.py:214
  258.4 2.4 fusion.5.row_back
  260.9 3.4 copy-done.2
  264.2 17.7 %outputs.1 = (f32[16,8,1024]{2,1,0:T(8,128)S(1)}, f32[16,8,1024]{2,1,0:T(8,128)S(1)}, f32[16,8,1024]{2,1,0:T(8,128)}, f32[16,8,1024]{2,1,0:T(8,128)}, f32[16,8,16]{2,1,0:T(8,128)}, /*index=5*/f32[16,8,16]{2,1,0:T(8,128)}) custom-call(f32[16,8,1024]{2,1,0:T(8,128)S(1)} %copy-done.8, f32[16,8,1024]{2,1,0:T(8,128)S(1)} %copy-done.5, ...), custom_call_target="tpu_custom_call" | custom-call | tf_op jit(solution)/shard_map/outputs/pallas_call | solution.py:199
  281.9 0.0 copy-start.22
  281.9 1.9 convolution_bitcast_fusion.1
  283.8 0.0 copy-done.17
  283.8 1.8 convolution_bitcast_fusion
  285.6 0.0 all-reduce.3.cloned.1.call-update
  285.6 1.0 copy-done.18
  286.7 1.1 fusion.4
  287.8 108.4 %all-reduce.3.cloned.1.call-done = (f32[512,1024]{0,1:T(8,128)}, f32[1024,512]{1,0:T(8,128)}) async-done(((f32[512,1024]{0,1:T(8,128)}, f32[1024,512]{1,0:T(8,128)}), (f32[512,1024]{0,1:T(8,128)}, f32[1024,512]{1,0:T(8,128)})) %all-reduce.3.cloned.1.call-update) | async-done | bytes 4194320 | tf_op jit(solution)/shard_map/psum | solution.py:269
  396.3 2.9 copy.27
  399.1 3.1 copy.44
  (22 shorter events, 0.1 us)
Async XLA Ops:
  7.2 4.5 %copy-start = (bf16[512,1024]{1,0:T(8,128)(2,1)S(1)}, bf16[512,1024]{1,0:T(8,128)(2,1)}, u32[]{:S(2)}) copy-start(bf16[512,1024]{1,0:T(8,128)(2,1)} %param.11) | copy-start | bytes 3145732
  7.2 4.5 %copy-start.20 = (bf16[16,8,512]{2,1,0:T(8,128)(2,1)S(1)}, bf16[16,8,512]{2,1,0:T(8,128)(2,1)}, u32[]{:S(2)}) copy-start(bf16[16,8,512]{2,1,0:T(8,128)(2,1)} %param.9) | copy-start | bytes 393220
  7.2 40.9 %all-gather.13.cloned.1.call-start = ((), (), s32[]{:S(2)}) async-start(), calls=%async_computation.1 | async-start | bytes 2621440 | tf_op jit(solution)/shard_map/all_gather | solution.py:214
  8.1 2.2 copy-start.19
  9.2 2.8 copy-start.13
  9.2 2.8 copy-start.14
  11.6 10.3 %copy-start.3 = (f32[16,8,1024]{2,1,0:T(8,128)}, f32[16,8,1024]{2,1,0:T(8,128)S(1)}, u32[]{:S(2)}) copy-start(f32[16,8,1024]{2,1,0:T(8,128)S(1)} %fusion.3.upstream) | copy-start | bytes 1572868
  12.0 27.2 %copy-start.6 = (f32[16,8,1024]{2,1,0:T(8,128)}, f32[16,8,1024]{2,1,0:T(8,128)S(1)}, u32[]{:S(2)}) copy-start(f32[16,8,1024]{2,1,0:T(8,128)S(1)} %fusion.1.signal) | copy-start | bytes 1572868
  20.1 1.0 copy-start.11
  21.1 0.8 copy-start.15
  21.9 109.1 %all-gather.11.cloned.1.call-start = ((), (), s32[]{:S(2)}) async-start(), calls=%async_computation | async-start | bytes 5242880 | tf_op jit(solution)/shard_map/all_gather | solution.py:214
  22.7 152.9 %all-gather.15.cloned.1.call-start = ((), (), s32[]{:S(2)}) async-start(), calls=%async_computation.2 | async-start | bytes 2621440 | tf_op jit(solution)/shard_map/all_gather | solution.py:214
  131.0 2.4 copy-start.4
  131.0 2.4 copy-start.7
  131.0 2.4 copy-start.9
  149.3 3.2 copy-start.1
  152.5 1.0 copy-start.12
  153.5 0.8 copy-start.16
  154.3 104.1 %all-gather.17.cloned.1.call-start = ((), (), s32[]{:S(2)}) async-start(), calls=%async_computation.3 | async-start | bytes 5242880 | tf_op jit(solution)/shard_map/all_gather | solution.py:214
  154.9 241.4 %all-reduce.3.cloned.1.call-start = ((), (), s32[]{:S(2)}) async-start(), calls=%async_computation.4 | async-start | bytes 8388608 | tf_op jit(solution)/shard_map/psum | solution.py:269
  258.4 2.4 copy-start.5
  258.4 2.5 copy-start.8
  258.4 2.5 copy-start.10
  260.9 3.4 copy-start.2
  264.2 17.7 %copy-start.21 = (bf16[16,8,512]{2,1,0:T(8,128)(2,1)S(1)}, bf16[16,8,512]{2,1,0:T(8,128)(2,1)}, u32[]{:S(2)}) copy-start(bf16[16,8,512]{2,1,0:T(8,128)(2,1)} %param.9) | copy-start | bytes 393220
  281.9 1.9 copy-start.17
  281.9 1.9 copy-start.22
  285.6 1.0 copy-start.18
Sparse Core Ops, SparseCore 0:
  22.0 25.9 all-gather.12
  50.2 80.7 all-gather.10
  154.4 21.1 all-gather.14
  177.6 80.7 all-gather.16
  285.8 110.4 all-reduce.2

commit v2 on v1

--- a/solution.py
+++ b/solution.py
@@ -9,6 +9,8 @@
 from jax.sharding import PartitionSpec as P
 
 LANES = 128
+CHUNKS = 8
+MESH = pl.DeviceIdType.MESH
 F32 = jnp.float32
 
 
@@ -208,17 +210,119 @@
     )(*args)
 
 
-def entering(total, product, axis, reverse):
+def chain_of(axis, step):
     count = lax.axis_size(axis)
     me = lax.axis_index(axis)
-    totals = lax.all_gather(total, axis)
-    products = lax.all_gather(product, axis)
-    state = jnp.zeros_like(total)
-    for turn in range(count - 1):
-        k = count - 1 - turn if reverse else turn
-        use = k > me if reverse else k < me
-        state = jnp.where(use, products[k] * state + totals[k], state)
-    return state
+    turn = me if step > 0 else count - 1 - me
+    after = lax.rem(me + step + count, count)
+    before = lax.rem(me - step + count, count)
+    return turn > 0, turn < count - 1, before, after
+
+
+def exchange_kernel(row_step, col_step, row_tot, row_prod, col_tot, col_prod, row_in, col_in,
+                    row_out, col_out, row_send, row_recv, col_send, col_recv):
+    row_has_before, row_has_after, row_before, row_after = chain_of("gc", row_step)
+    col_has_before, col_has_after, col_before, col_after = chain_of("gr", col_step)
+    barrier = pltpu.get_barrier_semaphore()
+
+    @pl.when(row_has_before)
+    def _():
+        pl.semaphore_signal(barrier, inc=1, device_id={"gc": row_before}, device_id_type=MESH)
+
+    @pl.when(col_has_before)
+    def _():
+        pl.semaphore_signal(barrier, inc=1, device_id={"gr": col_before}, device_id_type=MESH)
+
+    peers = row_has_after.astype(jnp.int32) + col_has_after.astype(jnp.int32)
+
+    @pl.when(peers > 0)
+    def _():
+        pl.semaphore_wait(barrier, peers)
+
+    row_part = row_tot.shape[0] // CHUNKS
+    col_part = col_tot.shape[0] // CHUNKS
+
+    def row_copy(k):
+        part = pl.ds(k * row_part, row_part)
+        return pltpu.make_async_remote_copy(
+            src_ref=row_out.at[part], dst_ref=row_in.at[part],
+            send_sem=row_send.at[k], recv_sem=row_recv.at[k],
+            device_id={"gc": row_after}, device_id_type=MESH,
+        )
+
+    def col_copy(k):
+        part = pl.ds(k * col_part, col_part)
+        return pltpu.make_async_remote_copy(
+            src_ref=col_out.at[part], dst_ref=col_in.at[part],
+            send_sem=col_send.at[k], recv_sem=col_recv.at[k],
+            device_id={"gr": col_after}, device_id_type=MESH,
+        )
+
+    @pl.when(jnp.logical_not(row_has_before))
+    def _():
+        row_in[...] = jnp.zeros_like(row_in)
+
+    @pl.when(jnp.logical_not(col_has_before))
+    def _():
+        col_in[...] = jnp.zeros_like(col_in)
+
+    def one(k, carry):
+        @pl.when(col_has_before)
+        def _():
+            col_copy(k).wait_recv()
+
+        @pl.when(col_has_after)
+        def _():
+            for p in range(col_part):
+                n = k * col_part + p
+                col_out[n] = col_prod[...] * col_in[n] + col_tot[n]
+            col_copy(k).start()
+
+        @pl.when(row_has_before)
+        def _():
+            row_copy(k).wait_recv()
+
+        @pl.when(row_has_after)
+        def _():
+            for p in range(row_part):
+                i = k * row_part + p
+                row_out[i] = row_prod[i] * row_in[i] + row_tot[i]
+            row_copy(k).start()
+
+        return carry
+
+    lax.fori_loop(0, CHUNKS, one, 0)
+
+    def finish(k, carry):
+        @pl.when(col_has_after)
+        def _():
+            col_copy(k).wait_send()
+
+        @pl.when(row_has_after)
+        def _():
+            row_copy(k).wait_send()
+
+        return carry
+
+    lax.fori_loop(0, CHUNKS, finish, 0)
+
+
+def exchange(name, number, row_step, col_step, row_tot, row_prod, col_tot, col_prod):
+    vmem = pl.BlockSpec(memory_space=pltpu.VMEM)
+    return pl.pallas_call(
+        functools.partial(exchange_kernel, row_step, col_step),
+        out_shape=[
+            jax.ShapeDtypeStruct(row_tot.shape, F32), jax.ShapeDtypeStruct(col_tot.shape, F32)
+        ],
+        in_specs=[vmem] * 4,
+        out_specs=[vmem] * 2,
+        scratch_shapes=[pltpu.VMEM(row_tot.shape, F32), pltpu.VMEM(col_tot.shape, F32)]
+        + [pltpu.SemaphoreType.DMA((CHUNKS,))] * 4,
+        compiler_params=pltpu.CompilerParams(
+            collective_id=number, has_side_effects=True, vmem_limit_bytes=32 * 2**20
+        ),
+        name=name,
+    )(row_tot, row_prod, col_tot, col_prod)
 
 
 def shards(features, out_grad, w_in, w_out, decay_row, decay_col, b_proj, c_proj, tissue):
@@ -247,14 +351,16 @@
         totals_kernel, "totals", scale, common, (4, 5),
         (row_edge, (rows, 1, inner), col_edge, (cols, inner)), (), (wide, wide),
     )
-    row_in = entering(row_tot, row_prod, "gc", False)
-    col_back = entering(col_back_tot, col_prod, "gr", True)
+    row_in, col_back = exchange(
+        "exchange_one", 0, 1, -1, row_tot, row_prod, col_back_tot, col_prod
+    )
     row_state, col_adj, col_tot, row_back_tot = call(
         states_kernel, "states", scale, (*common, row_in, col_back), (4, 5),
         (full, full, col_edge, row_edge), (), (wide, wide),
     )
-    col_in = entering(col_tot, col_prod, "gr", False)
-    row_back = entering(row_back_tot, row_prod, "gc", True)
+    row_back, col_in = exchange(
+        "exchange_two", 1, -1, 1, row_back_tot, row_prod, col_tot, col_prod
+    )
     mixed, signal_part, row_grad, col_grad, b_grad, c_grad = call(
         outputs_kernel, "outputs", scale,
         (*common, row_state, col_adj, row_in, col_in, row_back), (4, 5),

time: 409 us -> 265 us (0.65)
  waiting for transfers between devices: 293 us -> 112 us
  Pallas kernels: 41.6 us -> 117 us
  blocking collectives: 21.8 us -> 0 us
  other arithmetic: 13.7 us -> 2.85 us
  local copies, waits for them, and re-layouts: 18.2 us -> 11.1 us
    all_gather x4 -> x0, waiting for transfers between devices: 183 us -> none  [entering(): totals = lax.all_gather(total, axis)]
    pallas_call x0 -> x2, Pallas kernels: none -> 75.8 us  [exchange(): pl.pallas_call(functools.partial(exchange_kernel, row_step, col_step), ou...]
    all_gather x2 -> x0, blocking collectives: 21.8 us -> none  [entering(): products = lax.all_gather(product, axis)]
    select_n x4 -> x0, other arithmetic: 9.46 us -> none  [entering(): state = jnp.where(use, products[k] * state + totals[k], state)]
    unnamed x51 -> x20, local copies, waits for them, and re-layouts: 18.1 us -> 11 us
  transfers between devices with their start and end apart: 5 -> 1, of which waited for: 5 -> 1; matrix products, arithmetic and copies ran while one was open for 2% -> 0% of each run, Pallas kernels for 0% -> 0%
where the time goes in v2:
time: 265 us; the launch traced here: 264 us
  Pallas kernels  117 us (44%)
  waiting for transfers between devices  112 us (42%)
  between operations  14.2 us (5%)
  local copies, waits for them, and re-layouts  11.1 us (4%)
  matrix products  6.5 us (2%)
  other arithmetic  2.85 us (1%)
    psum x1, waiting for transfers between devices, shards(): w_in_grad, w_out_grad = lax.psum((w_in_part, w_out_part), ('gr', 'gc'))  112 us
    pallas_call x2, Pallas kernels, exchange(): pl.pallas_call(functools.partial(exchange_kernel, row_step, col_step), ou...  75.8 us
    pallas_call x3, Pallas kernels, call(): pl.pallas_call(functools.partial(kernel, scale), grid=(args[0].shape[-1]...  41.6 us
    unnamed x20, local copies, waits for them, and re-layouts  11 us
  transfers between devices with their start and end apart: 1, of which 1 were waited for; matrix products, arithmetic and copies ran while one was open for 0% of the time, Pallas kernels for 0%

profile of v2, /device:TPU:0, one launch (start us, length us, event | category | flops | bytes accessed | tf_op | source)
XLA Modules:
  0.0 264.5 jit_solution(694302401853749544)
XLA Ops:
  7.2 0.0 copy-start
  7.2 0.0 copy-start.6
  7.2 0.0 copy-start.7
  7.2 0.0 all-reduce.3.cloned.1.call-start
  7.2 0.8 convert_element_type.28
  8.1 0.1 copy.16
  8.2 1.0 convert_element_type.32.row_decay
  9.2 0.0 copy-start.3
  9.2 0.0 copy-start.4
  9.2 1.0 convert_element_type.33.col_decay
  10.2 0.0 copy-done.6
  10.2 1.4 fusion.3.upstream
  11.6 0.0 copy-done
  11.6 0.0 copy-done.7
  11.6 0.3 fusion.1.signal
  11.9 0.0 copy-done.3
  12.0 0.0 copy-done.4
  12.0 8.1 %totals.1 = (f32[16,16,1024]{2,1,0:T(8,128)S(1)}, f32[16,1,1024]{2,1,0:T(1,128)S(1)}, f32[16,8,1024]{2,1,0:T(8,128)S(1)}, f32[8,1024]{1,0:T(8,128)S(1)}) custom-call(f32[16,8,1024]{2,1,0:T(8,128)S(1)} %fusion.1.signal, f32[16,8,1024]{2,1,0:T(8,128)S(1)} %fusion.3.upstream, f32[16,8,1024]{2,1,0:T(8,128)S(1)} %convert_element_type.32.row_decay, ...), custom_call_target="tpu_custom_call" | custom-call | tf_op jit(solution)/shard_map/totals/pallas_call | solution.py:201
  20.1 30.3 %exchange_one.1 = (f32[16,16,1024]{2,1,0:T(8,128)S(1)}, f32[16,8,1024]{2,1,0:T(8,128)S(1)}) custom-call(f32[16,16,1024]{2,1,0:T(8,128)S(1)} %get-tuple-element.25.row_tot, f32[16,1,1024]{2,1,0:T(1,128)S(1)} %get-tuple-element.26.row_prod, f32[16,8,1024]{2,1,0:T(8,128)S(1)} %get-tuple-element.27.col_tot, f32[8,1024]{1,0:T(8,128)S(1)} %get-tuple-element.28.col_prod), custom_call_target="tpu_custom_call" | custom-call | tf_op jit(solution)/shard_map/exchange_one/pallas_call | solution.py:312
  50.3 15.9 %states.1 = (f32[16,16,8,1024]{3,2,1,0:T(8,128)S(1)}, f32[16,16,8,1024]{3,2,1,0:T(8,128)}, f32[16,8,1024]{2,1,0:T(8,128)S(1)}, f32[16,16,1024]{2,1,0:T(8,128)S(1)}) custom-call(f32[16,8,1024]{2,1,0:T(8,128)S(1)} %fusion.1.signal, f32[16,8,1024]{2,1,0:T(8,128)S(1)} %fusion.3.upstream, f32[16,8,1024]{2,1,0:T(8,128)S(1)} %convert_element_type.32.row_decay, ...), custom_call_target="tpu_custom_call" | custom-call | tf_op jit(solution)/shard_map/states/pallas_call | solution.py:201
  66.2 0.0 copy-start.1
  66.2 3.2 %copy-done.1 = f32[16,16,8,1024]{3,2,1,0:T(8,128)} copy-done((f32[16,16,8,1024]{3,2,1,0:T(8,128)}, f32[16,16,8,1024]{3,2,1,0:T(8,128)S(1)}, u32[]{:S(2)}) %copy-start.1) | copy-done | bytes 8388632
  69.4 45.5 %exchange_two.1 = (f32[16,16,1024]{2,1,0:T(8,128)S(1)}, f32[16,8,1024]{2,1,0:T(8,128)S(1)}) custom-call(f32[16,16,1024]{2,1,0:T(8,128)S(1)} %get-tuple-element.33.row_tot, f32[16,1,1024]{2,1,0:T(1,128)S(1)} %get-tuple-element.26.row_prod, f32[16,8,1024]{2,1,0:T(8,128)S(1)} %get-tuple-element.34.col_tot, f32[8,1024]{1,0:T(8,128)S(1)} %get-tuple-element.28.col_prod), custom_call_target="tpu_custom_call" | custom-call | tf_op jit(solution)/shard_map/exchange_two/pallas_call | solution.py:312
  115.0 0.0 copy-start.2
  115.0 3.4 %copy-done.2 = f32[16,16,8,1024]{3,2,1,0:T(8,128)S(1)} copy-done((f32[16,16,8,1024]{3,2,1,0:T(8,128)S(1)}, f32[16,16,8,1024]{3,2,1,0:T(8,128)}, u32[]{:S(2)}) %copy-start.2) | copy-done | bytes 8388632
  118.3 17.7 %outputs.1 = (f32[16,8,1024]{2,1,0:T(8,128)S(1)}, f32[16,8,1024]{2,1,0:T(8,128)S(1)}, f32[16,8,1024]{2,1,0:T(8,128)}, f32[16,8,1024]{2,1,0:T(8,128)}, f32[16,8,16]{2,1,0:T(8,128)}, /*index=5*/f32[16,8,16]{2,1,0:T(8,128)}) custom-call(f32[16,8,1024]{2,1,0:T(8,128)S(1)} %fusion.1.signal, f32[16,8,1024]{2,1,0:T(8,128)S(1)} %fusion.3.upstream, ...), custom_call_target="tpu_custom_call" | custom-call | tf_op jit(solution)/shard_map/outputs/pallas_call | solution.py:201
  136.0 0.0 copy-start.8
  136.0 1.9 convolution_bitcast_fusion.1
  137.9 0.0 copy-done.8
  137.9 1.8 convolution_bitcast_fusion
  139.7 0.0 all-reduce.3.cloned.1.call-update
  139.7 1.1 fusion.4
  140.9 112.4 %all-reduce.3.cloned.1.call-done = (f32[512,1024]{0,1:T(8,128)}, f32[1024,512]{1,0:T(8,128)}) async-done(((f32[512,1024]{0,1:T(8,128)}, f32[1024,512]{1,0:T(8,128)}), (f32[512,1024]{0,1:T(8,128)}, f32[1024,512]{1,0:T(8,128)})) %all-reduce.3.cloned.1.call-update) | async-done | bytes 4194320 | tf_op jit(solution)/shard_map/psum | solution.py:375
  253.3 0.0 copy-start.5
  253.3 3.0 %copy.21 = f32[512,1024]{1,0:T(8,128)} copy(f32[512,1024]{0,1:T(8,128)} %get-tuple-element.50) | data formatting | bytes 4194304
  256.3 0.0 copy-done.5
  256.3 1.3 copy.28
Async XLA Ops:
  7.2 4.4 %copy-start = (bf16[512,1024]{1,0:T(8,128)(2,1)S(1)}, bf16[512,1024]{1,0:T(8,128)(2,1)}, u32[]{:S(2)}) copy-start(bf16[512,1024]{1,0:T(8,128)(2,1)} %param.11) | copy-start | bytes 3145732
  7.2 3.0 %copy-start.6 = (bf16[1024,512]{1,0:T(8,128)(2,1)S(1)}, bf16[1024,512]{1,0:T(8,128)(2,1)}, u32[]{:S(2)}) copy-start(bf16[1024,512]{1,0:T(8,128)(2,1)} %param.12) | copy-start | bytes 3145732
  7.2 4.4 %copy-start.7 = (bf16[16,8,512]{2,1,0:T(8,128)(2,1)S(1)}, bf16[16,8,512]{2,1,0:T(8,128)(2,1)}, u32[]{:S(2)}) copy-start(bf16[16,8,512]{2,1,0:T(8,128)(2,1)} %param.9) | copy-start | bytes 393220
  7.2 246.1 %all-reduce.3.cloned.1.call-start = ((), (), s32[]{:S(2)}) async-start(), calls=%async_computation | async-start | bytes 8388608 | tf_op jit(solution)/shard_map/psum | solution.py:375
  9.2 2.8 %copy-start.3 = (f32[16,8,16]{2,1,0:T(8,128)S(1)}, f32[16,8,16]{2,1,0:T(8,128)}, u32[]{:S(2)}) copy-start(f32[16,8,16]{2,1,0:T(8,128)} %b_proj.5) | copy-start | bytes 24580
  9.2 2.8 %copy-start.4 = (f32[16,8,16]{2,1,0:T(8,128)S(1)}, f32[16,8,16]{2,1,0:T(8,128)}, u32[]{:S(2)}) copy-start(f32[16,8,16]{2,1,0:T(8,128)} %c_proj.5) | copy-start | bytes 24580
  66.2 3.2 %copy-start.1 = (f32[16,16,8,1024]{3,2,1,0:T(8,128)}, f32[16,16,8,1024]{3,2,1,0:T(8,128)S(1)}, u32[]{:S(2)}) copy-start(f32[16,16,8,1024]{3,2,1,0:T(8,128)S(1)} %get-tuple-element.31.row_state) | copy-start | bytes 25165828
  115.0 3.4 %copy-start.2 = (f32[16,16,8,1024]{3,2,1,0:T(8,128)S(1)}, f32[16,16,8,1024]{3,2,1,0:T(8,128)}, u32[]{:S(2)}) copy-start(f32[16,16,8,1024]{3,2,1,0:T(8,128)} %copy-done.1) | copy-start | bytes 25165828
  136.0 1.9 copy-start.8
  253.3 3.0 %copy-start.5 = (f32[1024,512]{1,0:T(8,128)S(1)}, f32[1024,512]{1,0:T(8,128)}, u32[]{:S(2)}) copy-start(f32[1024,512]{1,0:T(8,128)} %get-tuple-element.54) | copy-start | bytes 6291460
Sparse Core Ops, SparseCore 0:
  139.8 113.3 all-reduce.2

commit v3 on v1

--- a/solution.py
+++ b/solution.py
@@ -9,6 +9,8 @@
 from jax.sharding import PartitionSpec as P
 
 LANES = 128
+CHUNKS = 8
+MESH = pl.DeviceIdType.MESH
 F32 = jnp.float32
 
 
@@ -131,55 +133,75 @@
         col_tot[n] = out[n]
 
 
-def outputs_kernel(scale, signal, upstream, row_decay, col_decay, b_proj, c_proj,
-                   row_state, col_adj, row_in, col_in, row_back,
-                   mixed, signal_part, row_grad, col_grad, b_grad, c_grad,
-                   b_wide, c_wide, b_sum, c_sum):
-    rows, cols, states = b_proj.shape
+def col_outputs_kernel(scale, upstream, col_decay, c_proj, row_state, col_adj, col_in,
+                       mixed, col_grad, c_grad, c_wide, c_sum):
+    rows, cols, states = c_proj.shape
 
     @pl.when(pl.program_id(0) == 0)
     def _():
-        spread(b_proj, b_wide, scale)
         spread(c_proj, c_wide, 1.0)
-        b_sum[...] = jnp.zeros_like(b_sum)
         c_sum[...] = jnp.zeros_like(c_sum)
 
     def one(i, column):
         down = col_decay[i]
-        source = signal[i]
         up = upstream[i]
-        steps, product = back_weights(row_decay[i])
-        first = place((cols, LANES)) == 0
         mixed_now = jnp.zeros((cols, LANES), F32)
-        signal_now, row_now, col_now = mixed_now, mixed_now, mixed_now
+        col_now = mixed_now
         updated = []
         for n in range(states):
-            state = row_state[i, n]
-            adjoint = col_adj[i, n]
-            col_now = col_now + adjoint * column[n]
-            fresh = down * column[n] + state
+            col_now = col_now + col_adj[i, n] * column[n]
+            fresh = down * column[n] + row_state[i, n]
             updated.append(fresh)
             mixed_now = mixed_now + c_wide[i, n] * fresh
             c_sum[i, n] += up * fresh
-            row_adj = run_scan(steps, adjoint) + product * row_back[i, n : n + 1, :]
-            before = jnp.where(first, row_in[i, n : n + 1, :], pltpu.roll(state, 1, 0))
+        mixed[i] = mixed_now
+        col_grad[i] = col_now
+        return tuple(updated)
+
+    lax.fori_loop(0, rows, one, tuple(col_in[n] for n in range(states)))
+
+    @pl.when(pl.program_id(0) == pl.num_programs(0) - 1)
+    def _():
+        def finish(i, carry):
+            for n in range(states):
+                c_grad[i, :, n : n + 1] = jnp.sum(c_sum[i, n], axis=1, keepdims=True)
+            return carry
+
+        lax.fori_loop(0, rows, finish, 0)
+
+
+def row_outputs_kernel(scale, signal, row_decay, b_proj, row_state, col_adj, row_in, row_back,
+                       signal_part, row_grad, b_grad, b_wide, b_sum):
+    rows, cols, states = b_proj.shape
+
+    @pl.when(pl.program_id(0) == 0)
+    def _():
+        spread(b_proj, b_wide, scale)
+        b_sum[...] = jnp.zeros_like(b_sum)
+
+    def one(i, carry):
+        source = signal[i]
+        steps, product = back_weights(row_decay[i])
+        first = place((cols, LANES)) == 0
+        signal_now = jnp.zeros((cols, LANES), F32)
+        row_now = signal_now
+        for n in range(states):
+            row_adj = run_scan(steps, col_adj[i, n]) + product * row_back[i, n : n + 1, :]
+            before = jnp.where(first, row_in[i, n : n + 1, :], pltpu.roll(row_state[i, n], 1, 0))
             row_now = row_now + row_adj * before
             signal_now = signal_now + b_wide[i, n] * row_adj
             b_sum[i, n] += source * row_adj
-        mixed[i] = mixed_now
         signal_part[i] = signal_now
         row_grad[i] = row_now
-        col_grad[i] = col_now
-        return tuple(updated)
-
-    lax.fori_loop(0, rows, one, tuple(col_in[n] for n in range(states)))
+        return carry
+
+    lax.fori_loop(0, rows, one, 0)
 
     @pl.when(pl.program_id(0) == pl.num_programs(0) - 1)
     def _():
         def finish(i, carry):
             for n in range(states):
                 b_grad[i, :, n : n + 1] = scale * jnp.sum(b_sum[i, n], axis=1, keepdims=True)
-                c_grad[i, :, n : n + 1] = jnp.sum(c_sum[i, n], axis=1, keepdims=True)
             return carry
 
         lax.fori_loop(0, rows, finish, 0)
@@ -208,17 +230,97 @@
     )(*args)
 
 
-def entering(total, product, axis, reverse):
+def chain_of(axis, step):
     count = lax.axis_size(axis)
     me = lax.axis_index(axis)
-    totals = lax.all_gather(total, axis)
-    products = lax.all_gather(product, axis)
-    state = jnp.zeros_like(total)
-    for turn in range(count - 1):
-        k = count - 1 - turn if reverse else turn
-        use = k > me if reverse else k < me
-        state = jnp.where(use, products[k] * state + totals[k], state)
-    return state
+    turn = me if step > 0 else count - 1 - me
+    after = lax.rem(me + step + count, count)
+    before = lax.rem(me - step + count, count)
+    return turn > 0, turn < count - 1, before, after
+
+
+def exchange_kernel(chains, *refs):
+    count = len(chains)
+    total, product = refs[0 : 2 * count : 2], refs[1 : 2 * count : 2]
+    arrived = refs[2 * count : 3 * count]
+    leaving = refs[3 * count : 4 * count]
+    send, recv = refs[4 * count : 5 * count], refs[5 * count :]
+    places = [chain_of(axis, step) for axis, step in chains]
+    barrier = pltpu.get_barrier_semaphore()
+    peers = 0
+    for (axis, _), (has_before, has_after, before, _) in zip(chains, places):
+        peers = peers + has_after.astype(jnp.int32)
+
+        @pl.when(has_before)
+        def _(axis=axis, before=before):
+            pl.semaphore_signal(barrier, inc=1, device_id={axis: before}, device_id_type=MESH)
+
+    @pl.when(peers > 0)
+    def _():
+        pl.semaphore_wait(barrier, peers)
+
+    def copy(c, k):
+        size = total[c].shape[0] // CHUNKS
+        part = pl.ds(k * size, size)
+        return pltpu.make_async_remote_copy(
+            src_ref=leaving[c].at[part], dst_ref=arrived[c].at[part],
+            send_sem=send[c].at[k], recv_sem=recv[c].at[k],
+            device_id={chains[c][0]: places[c][3]}, device_id_type=MESH,
+        )
+
+    for c in range(count):
+
+        @pl.when(jnp.logical_not(places[c][0]))
+        def _(c=c):
+            arrived[c][...] = jnp.zeros_like(arrived[c])
+
+    def one(k, carry):
+        for c in range(count):
+
+            @pl.when(places[c][0])
+            def _(c=c):
+                copy(c, k).wait_recv()
+
+            @pl.when(places[c][1])
+            def _(c=c):
+                size = total[c].shape[0] // CHUNKS
+                for p in range(size):
+                    i = k * size + p
+                    weight = product[c][i] if len(product[c].shape) == 3 else product[c][...]
+                    leaving[c][i] = weight * arrived[c][i] + total[c][i]
+                copy(c, k).start()
+
+        return carry
+
+    lax.fori_loop(0, CHUNKS, one, 0)
+
+    def finish(k, carry):
+        for c in range(count):
+
+            @pl.when(places[c][1])
+            def _(c=c):
+                copy(c, k).wait_send()
+
+        return carry
+
+    lax.fori_loop(0, CHUNKS, finish, 0)
+
+
+def exchange(name, number, chains, *args):
+    vmem = pl.BlockSpec(memory_space=pltpu.VMEM)
+    shapes = [a.shape for a in args[::2]]
+    return pl.pallas_call(
+        functools.partial(exchange_kernel, chains),
+        out_shape=[jax.ShapeDtypeStruct(a, F32) for a in shapes],
+        in_specs=[vmem] * len(args),
+        out_specs=[vmem] * len(shapes),
+        scratch_shapes=[pltpu.VMEM(a, F32) for a in shapes]
+        + [pltpu.SemaphoreType.DMA((CHUNKS,))] * (2 * len(shapes)),
+        compiler_params=pltpu.CompilerParams(
+            collective_id=number, has_side_effects=True, vmem_limit_bytes=32 * 2**20
+        ),
+        name=name,
+    )(*args)
 
 
 def shards(features, out_grad, w_in, w_out, decay_row, decay_col, b_proj, c_proj, tissue):
@@ -247,26 +349,36 @@
         totals_kernel, "totals", scale, common, (4, 5),
         (row_edge, (rows, 1, inner), col_edge, (cols, inner)), (), (wide, wide),
     )
-    row_in = entering(row_tot, row_prod, "gc", False)
-    col_back = entering(col_back_tot, col_prod, "gr", True)
+    row_in, col_back = exchange(
+        "exchange_one", 0, (("gc", 1), ("gr", -1)), row_tot, row_prod, col_back_tot, col_prod
+    )
     row_state, col_adj, col_tot, row_back_tot = call(
         states_kernel, "states", scale, (*common, row_in, col_back), (4, 5),
         (full, full, col_edge, row_edge), (), (wide, wide),
     )
-    col_in = entering(col_tot, col_prod, "gr", False)
-    row_back = entering(row_back_tot, row_prod, "gc", True)
-    mixed, signal_part, row_grad, col_grad, b_grad, c_grad = call(
-        outputs_kernel, "outputs", scale,
-        (*common, row_state, col_adj, row_in, col_in, row_back), (4, 5),
-        (cell, cell, cell, cell, b_proj.shape, c_proj.shape), (4, 5), (wide, wide, wide, wide),
+    (col_in,) = exchange("exchange_col", 1, (("gr", 1),), col_tot, col_prod)
+    signal, upstream, row_decay, col_decay = common[:4]
+    mixed, col_grad, c_grad = call(
+        col_outputs_kernel, "col_outputs", scale,
+        (upstream, col_decay, c_proj, row_state, col_adj, col_in), (2,),
+        (cell, cell, c_proj.shape), (2,), (wide, wide),
     )
     mixed = mixed.astype(jnp.bfloat16).reshape(cells, inner)
+    w_out_part = lax.dot_general(mixed, grad, contract_first, preferred_element_type=F32)
+    w_out_part, row_back_tot = lax.optimization_barrier((w_out_part, row_back_tot))
+    w_out_grad = lax.psum(w_out_part, ("gr", "gc"))
+    (row_back,) = exchange("exchange_row", 2, (("gc", -1),), row_back_tot, row_prod)
+    signal_part, row_grad, b_grad = call(
+        row_outputs_kernel, "row_outputs", scale,
+        (signal, row_decay, b_proj, row_state, col_adj, row_in, row_back), (2,),
+        (cell, cell, b_proj.shape), (2,), (wide, wide),
+    )
     signal_grad = (keep * signal_part).astype(jnp.bfloat16).reshape(cells, inner)
+    w_in_part = lax.dot_general(feat, signal_grad, contract_first, preferred_element_type=F32)
+    w_in_part, w_out_grad = lax.optimization_barrier((w_in_part, w_out_grad))
+    w_in_grad = lax.psum(w_in_part, ("gc", "gr"))
     feat_grad = lax.dot_general(signal_grad, w_in, contract_last, preferred_element_type=F32)
     feat_grad = feat_grad.astype(jnp.bfloat16).reshape(rows, cols, width)
-    w_in_part = lax.dot_general(feat, signal_grad, contract_first, preferred_element_type=F32)
-    w_out_part = lax.dot_general(mixed, grad, contract_first, preferred_element_type=F32)
-    w_in_grad, w_out_grad = lax.psum((w_in_part, w_out_part), ("gr", "gc"))
     return (feat_grad, w_in_grad, w_out_grad, row_grad, col_grad, b_grad, c_grad)
 
 

time: 409 us -> 324 us (0.79)
  waiting for transfers between devices: 293 us -> 148 us
  Pallas kernels: 41.6 us -> 135 us
  blocking collectives: 21.8 us -> 0 us
  other arithmetic: 13.7 us -> 2.85 us
    all_gather x4 -> x0, waiting for transfers between devices: 183 us -> none  [entering(): totals = lax.all_gather(total, axis)]
    pallas_call x0 -> x3, Pallas kernels: none -> 85.7 us  [exchange(): pl.pallas_call(functools.partial(exchange_kernel, chains), out_shape=[jax...]
    psum x1 -> x2, waiting for transfers between devices: 108 us -> 148 us  [the longest x1 100 us: shards(): w_in_grad = lax.psum(w_in_part, ('gc', 'gr'))]
    all_gather x2 -> x0, blocking collectives: 21.8 us -> none  [entering(): products = lax.all_gather(product, axis)]
    select_n x4 -> x0, other arithmetic: 9.46 us -> none  [entering(): state = jnp.where(use, products[k] * state + totals[k], state)]
    pallas_call x3 -> x4, Pallas kernels: 41.6 us -> 49.2 us  [call(): pl.pallas_call(functools.partial(kernel, scale), grid=(args[0].shape[-1]...]
    unnamed x51 -> x30, local copies, waits for them, and re-layouts: 18.1 us -> 16.2 us
  transfers between devices with their start and end apart: 5 -> 2, of which waited for: 5 -> 2; matrix products, arithmetic and copies ran while one was open for 2% -> 1% of each run, Pallas kernels for 0% -> 22%
where the time goes in v3:
time: 324 us; the launch traced here: 323 us
  waiting for transfers between devices  148 us (46%)
  Pallas kernels  135 us (42%)
  local copies, waits for them, and re-layouts  16.3 us (5%)
  between operations  14.2 us (4%)
  matrix products  6.5 us (2%)
    psum x1, waiting for transfers between devices, shards(): w_in_grad = lax.psum(w_in_part, ('gc', 'gr'))  100 us
    pallas_call x3, Pallas kernels, exchange(): pl.pallas_call(functools.partial(exchange_kernel, chains), out_shape=[jax...  85.7 us
    pallas_call x4, Pallas kernels, call(): pl.pallas_call(functools.partial(kernel, scale), grid=(args[0].shape[-1]...  49.2 us
    psum x1, waiting for transfers between devices, shards(): w_out_grad = lax.psum(w_out_part, ('gr', 'gc'))  47.6 us
    unnamed x30, local copies, waits for them, and re-layouts  16.2 us
  transfers between devices with their start and end apart: 2, of which 2 were waited for; matrix products, arithmetic and copies ran while one was open for 1% of the time, Pallas kernels for 22%

profile of v3, /device:TPU:0, one launch (start us, length us, event | category | flops | bytes accessed | tf_op | source)
XLA Modules:
  0.0 323.0 jit_solution(3052998566249453032)
XLA Ops:
  7.2 0.0 copy-start
  7.2 0.0 copy-start.11
  7.2 0.0 copy-start.13
  7.2 0.0 all-reduce.3.cloned.1.call-start
  7.2 0.8 convert_element_type.28
  8.1 0.1 copy.16
  8.2 1.0 convert_element_type.31.row_decay
  9.2 0.0 copy-start.6
  9.2 0.0 copy-start.7
  9.2 1.0 convert_element_type.33.col_decay
  10.2 0.0 copy-done.11
  10.2 1.4 fusion.3.upstream
  11.6 0.0 copy-done
  11.6 0.0 copy-done.13
  11.6 0.3 fusion.1.signal
  11.9 0.0 copy-done.6
  12.0 0.0 copy-done.7
  12.0 8.1 %totals.1 = (f32[16,16,1024]{2,1,0:T(8,128)S(1)}, f32[16,1,1024]{2,1,0:T(1,128)S(1)}, f32[16,8,1024]{2,1,0:T(8,128)S(1)}, f32[8,1024]{1,0:T(8,128)S(1)}) custom-call(f32[16,8,1024]{2,1,0:T(8,128)S(1)} %fusion.1.signal, f32[16,8,1024]{2,1,0:T(8,128)S(1)} %fusion.3.upstream, f32[16,8,1024]{2,1,0:T(8,128)S(1)} %convert_element_type.31.row_decay, ...), custom_call_target="tpu_custom_call" | custom-call | tf_op jit(solution)/shard_map/totals/pallas_call | solution.py:221
  20.1 27.5 %exchange_one.1 = (f32[16,16,1024]{2,1,0:T(8,128)S(1)}, f32[16,8,1024]{2,1,0:T(8,128)S(1)}) custom-call(f32[16,16,1024]{2,1,0:T(8,128)S(1)} %get-tuple-element.27.refs_0_, f32[16,1,1024]{2,1,0:T(1,128)S(1)} %get-tuple-element.28.refs_1_, f32[16,8,1024]{2,1,0:T(8,128)S(1)} %get-tuple-element.29.refs_2_, f32[8,1024]{1,0:T(8,128)S(1)} %get-tuple-element.30.refs_3_.refs_1_), custom_call_target="tpu_custom_call" | custom-call | tf_op jit(solution)/shard_map/exchange_one/pallas_call | solution.py:312
  47.5 15.9 %states.1 = (f32[16,16,8,1024]{3,2,1,0:T(8,128)S(1)}, f32[16,16,8,1024]{3,2,1,0:T(8,128)}, f32[16,8,1024]{2,1,0:T(8,128)S(1)}, f32[16,16,1024]{2,1,0:T(8,128)S(1)}) custom-call(f32[16,8,1024]{2,1,0:T(8,128)S(1)} %fusion.1.signal, f32[16,8,1024]{2,1,0:T(8,128)S(1)} %fusion.3.upstream, f32[16,8,1024]{2,1,0:T(8,128)S(1)} %convert_element_type.31.row_decay, ...), custom_call_target="tpu_custom_call" | custom-call | tf_op jit(solution)/shard_map/states/pallas_call | solution.py:221
  63.4 0.0 copy-start.1
  63.4 3.2 %copy-done.1 = f32[16,16,8,1024]{3,2,1,0:T(8,128)} copy-done((f32[16,16,8,1024]{3,2,1,0:T(8,128)}, f32[16,16,8,1024]{3,2,1,0:T(8,128)S(1)}, u32[]{:S(2)}) %copy-start.1) | copy-done | bytes 8388632
  66.6 0.0 copy-start.4
  66.6 1.7 exchange_col.1.col_in
  68.4 0.0 copy-done.4
  68.4 0.0 copy-start.2
  68.4 3.4 %copy-done.2 = f32[16,16,8,1024]{3,2,1,0:T(8,128)S(1)} copy-done((f32[16,16,8,1024]{3,2,1,0:T(8,128)S(1)}, f32[16,16,8,1024]{3,2,1,0:T(8,128)}, u32[]{:S(2)}) %copy-start.2) | copy-done | bytes 8388632
  71.8 0.0 copy-start.12
  71.8 11.6 %col_outputs.1 = (f32[16,8,1024]{2,1,0:T(8,128)S(1)}, f32[16,8,1024]{2,1,0:T(8,128)}, f32[16,8,16]{2,1,0:T(8,128)}) custom-call(f32[16,8,1024]{2,1,0:T(8,128)S(1)} %fusion.3.upstream, f32[16,8,1024]{2,1,0:T(8,128)S(1)} %convert_element_type.33.col_decay, f32[16,8,16]{2,1,0:T(8,128)S(1)} %copy-done.6, f32[16,16,8,1024]{3,2,1,0:T(8,128)S(1)} %copy-done.2, ...), custom_call_target="tpu_custom_call" | custom-call | tf_op jit(solution)/shard_map/col_outputs/pallas_call | solution.py:221
  83.4 0.0 copy-done.12
  83.4 1.8 convolution_bitcast_fusion.1
  85.2 0.0 all-reduce.3.cloned.1.call-update
  85.2 0.0 all-reduce.5.cloned.1.call-start
  85.3 0.0 copy-start.5
  85.3 1.2 copy-done.5
  86.5 56.5 %exchange_row.1.row_back = f32[16,16,1024]{2,1,0:T(8,128)S(1)} custom-call(f32[16,16,1024]{2,1,0:T(8,128)S(1)} %copy-done.5, f32[16,1,1024]{2,1,0:T(1,128)S(1)} %get-tuple-element.28.refs_1_), custom_call_target="tpu_custom_call" | custom-call | tf_op jit(solution)/shard_map/exchange_row/pallas_call | solution.py:312
  143.0 0.0 copy-start.3
  143.0 3.4 %copy-done.3 = f32[16,16,8,1024]{3,2,1,0:T(8,128)S(1)} copy-done((f32[16,16,8,1024]{3,2,1,0:T(8,128)S(1)}, f32[16,16,8,1024]{3,2,1,0:T(8,128)}, u32[]{:S(2)}) %copy-start.3) | copy-done | bytes 8388632
  146.4 13.6 %row_outputs.1 = (f32[16,8,1024]{2,1,0:T(8,128)S(1)}, f32[16,8,1024]{2,1,0:T(8,128)}, f32[16,8,16]{2,1,0:T(8,128)}) custom-call(f32[16,8,1024]{2,1,0:T(8,128)S(1)} %fusion.1.signal, f32[16,8,1024]{2,1,0:T(8,128)S(1)} %convert_element_type.31.row_decay, f32[16,8,16]{2,1,0:T(8,128)S(1)} %copy-done.7, f32[16,16,8,1024]{3,2,1,0:T(8,128)S(1)} %copy-done.3, ...), custom_call_target="tpu_custom_call" | custom-call | tf_op jit(solution)/shard_map/row_outputs/pallas_call | solution.py:221
  160.0 0.0 copy-start.8
  160.0 0.8 copy-done.8
  160.8 1.9 convolution_bitcast_fusion
  162.6 0.0 copy-start.9
  162.6 47.6 %all-reduce.3.cloned.1.call-done = f32[1024,512]{1,0:T(8,128)} async-done(((f32[1024,512]{1,0:T(8,128)}), f32[1024,512]{1,0:T(8,128)}) %all-reduce.3.cloned.1.call-update) | async-done | bytes 2097168 | tf_op jit(solution)/shard_map/psum | solution.py:369
  210.3 0.0 all-reduce.5.cloned.1.call-update
  210.3 0.0 copy-done.9
  210.3 1.1 fusion.4
  211.4 0.0 copy-start.10
  211.4 100.5 %all-reduce.5.cloned.1.call-done = f32[512,1024]{0,1:T(8,128)} async-done(((f32[512,1024]{0,1:T(8,128)}), f32[512,1024]{0,1:T(8,128)}) %all-reduce.5.cloned.1.call-update) | async-done | bytes 2097168 | tf_op jit(solution)/shard_map/psum | solution.py:379
  311.9 2.9 copy.21
  314.8 0.0 copy-done.10
  314.8 1.3 copy.28
Async XLA Ops:
  7.2 4.4 %copy-start = (bf16[512,1024]{1,0:T(8,128)(2,1)S(1)}, bf16[512,1024]{1,0:T(8,128)(2,1)}, u32[]{:S(2)}) copy-start(bf16[512,1024]{1,0:T(8,128)(2,1)} %param.11) | copy-start | bytes 3145732
  7.2 3.0 copy-start.11
  7.2 4.4 %copy-start.13 = (bf16[16,8,512]{2,1,0:T(8,128)(2,1)S(1)}, bf16[16,8,512]{2,1,0:T(8,128)(2,1)}, u32[]{:S(2)}) copy-start(bf16[16,8,512]{2,1,0:T(8,128)(2,1)} %param.9) | copy-start | bytes 393220
  7.2 203.1 %all-reduce.3.cloned.1.call-start = ((), (), s32[]{:S(2)}) async-start(), calls=%async_computation | async-start | bytes 4194304 | tf_op jit(solution)/shard_map/psum | solution.py:369
  9.2 2.8 copy-start.6
  9.2 2.8 copy-start.7
  63.4 3.2 %copy-start.1 = (f32[16,16,8,1024]{3,2,1,0:T(8,128)}, f32[16,16,8,1024]{3,2,1,0:T(8,128)S(1)}, u32[]{:S(2)}) copy-start(f32[16,16,8,1024]{3,2,1,0:T(8,128)S(1)} %get-tuple-element.33.row_state) | copy-start | bytes 25165828
  66.6 1.7 copy-start.4
  68.4 3.4 %copy-start.2 = (f32[16,16,8,1024]{3,2,1,0:T(8,128)S(1)}, f32[16,16,8,1024]{3,2,1,0:T(8,128)}, u32[]{:S(2)}) copy-start(f32[16,16,8,1024]{3,2,1,0:T(8,128)} %copy-done.1) | copy-start | bytes 25165828
  71.8 11.6 %copy-start.12 = (bf16[16,8,512]{2,1,0:T(8,128)(2,1)S(1)}, bf16[16,8,512]{2,1,0:T(8,128)(2,1)}, u32[]{:S(2)}) copy-start(bf16[16,8,512]{2,1,0:T(8,128)(2,1)} %param.10) | copy-start | bytes 393220
  85.2 226.7 %all-reduce.5.cloned.1.call-start = ((), (), s32[]{:S(2)}) async-start(), calls=%async_computation.1 | async-start | bytes 4194304 | tf_op jit(solution)/shard_map/psum | solution.py:379
  85.3 1.2 copy-start.5
  143.0 3.4 %copy-start.3 = (f32[16,16,8,1024]{3,2,1,0:T(8,128)S(1)}, f32[16,16,8,1024]{3,2,1,0:T(8,128)}, u32[]{:S(2)}) copy-start(f32[16,16,8,1024]{3,2,1,0:T(8,128)} %copy-done.1) | copy-start | bytes 25165828
  160.0 0.8 copy-start.8
  162.6 47.7 %copy-start.9 = (f32[16,8,1024]{2,1,0:T(8,128)S(1)}, f32[16,8,1024]{2,1,0:T(8,128)}, u32[]{:S(2)}) copy-start(f32[16,8,1024]{2,1,0:T(8,128)} %copy-done.8) | copy-start | bytes 1572868
  211.4 103.4 %copy-start.10 = (f32[1024,512]{1,0:T(8,128)S(1)}, f32[1024,512]{1,0:T(8,128)}, u32[]{:S(2)}) copy-start(f32[1024,512]{1,0:T(8,128)} %all-reduce.3.cloned.1.call-done) | copy-start | bytes 6291460
Sparse Core Ops, SparseCore 0:
  85.3 124.8 all-reduce.2
  214.8 97.0 all-reduce.4
